TPU v7x, 512 devices: a whole 4x8x8 slice. The times are simulated.
512 devices in a mesh: row: 16 (over y_lo, z), col: 32 (over x, y_hi, core).
Axes of the slice: x: 4, y: 8 (y_hi: 4, y_lo: 2; y = y_hi * 2 + y_lo), z: 8, core: 2. Of those that a mesh axis runs over, the one named last changes fastest.
Arguments:
- iterate: bfloat16 [3584, 18432], P('row', 'col'), as said below
Outputs:
- update: bfloat16 [3584, 18432], P('row', 'col')
Inputs may be any that keep to these rules, and one draw needn't show every extreme that they name: An iterate of the orthogonalization, with spectral norm of order one.
All inputs are finite; a program needn't handle non-finite values.
Results may differ from a plain program's by a relative error of at most 0.018.
Values may be sent and summed in bfloat16 or wider, within the bound.
A program may use at most 64 MiB of HBM per device.

v0:
```python
import math

import jax
import jax.numpy as jnp
from jax import lax
from jax.sharding import PartitionSpec as P

N = 18432


coef_a = 3.4445
coef_b = -4.775
coef_c = 2.0315


def per_device(iterate):
    contract = (((1,), (1,)), ((), ()))
    partial_value = lax.dot_general(
        iterate,
        lax.all_gather(iterate, "row", axis=0, tiled=True),
        contract,
        preferred_element_type=jnp.float32,
    )
    partial_value = partial_value.astype(jnp.bfloat16)
    gram_tile = (
        lax.psum_scatter(partial_value, "col", scatter_dimension=1, tiled=True)
        .astype(jnp.float32)
        .astype(jnp.bfloat16)
    )
    gram_panel = lax.all_gather(gram_tile, "col", axis=1, tiled=True)
    squared = jnp.dot(
        gram_panel,
        lax.all_gather(gram_tile, "row", axis=0, tiled=True),
        preferred_element_type=jnp.float32,
    )
    factor = (coef_b * gram_tile.astype(jnp.float32) + coef_c * squared).astype(jnp.bfloat16)
    factor_panel = lax.all_gather(factor, "col", axis=1, tiled=True)
    product = jnp.dot(
        factor_panel,
        lax.all_gather(iterate, "row", axis=0, tiled=True),
        preferred_element_type=jnp.float32,
    )
    result = coef_a * iterate.astype(jnp.float32) + product
    return (math.sqrt(N) * result).astype(jnp.bfloat16)


def solution(mesh):
    return jax.shard_map(
        per_device,
        mesh=mesh,
        in_specs=(P("row", "col"),),
        out_specs=P("row", "col"),
        check_vma=False,
    )
```

profile of v0, /device:TPU:1, one launch (start us, length us, event | category | flops | bytes accessed | tf_op | source)
XLA Modules:
  0.0 329.7 jit_solution(10073282750905723207)
XLA Ops:
  6.5 0.0 all-gather.4.cloned.1.call-start
  6.5 0.7 all-gather.4.cloned.1.call-update
  7.3 0.0 reduce-scatter.4.cloned.1.call-start
  7.3 80.2 %all-gather.4.cloned.1.call-done = bf16[3584,576]{1,0:T(8,128)(2,1)} async-done(((bf16[224,576]{1,0:T(8,128)(2,1)}), bf16[3584,576]{1,0:T(8,128)(2,1)}) %all-gather.4.cloned.1.call-update) | async-done | bytes 4128784 | tf_op jit(solution)/shard_map/all_gather | solution.py:20
  87.5 4.1 %convolution_convert_fusion = bf16[224,3584]{1,0:T(8,128)(2,1)S(1)} fusion(bf16[224,576]{1,0:T(8,128)(2,1)} %param.1, bf16[3584,576]{1,0:T(8,128)(2,1)} %all-gather.4.cloned.1.call-done), kind=kOutput, calls=%fused_computation | convolution fusion | flops 925646848 | bytes 5992448 | tf_op jit(solution)/shard_map/dot_general | solution.py:18
  91.6 2.3 copy.4
  93.8 0.0 reduce-scatter.4.cloned.1.call-update
  93.9 0.0 all-gather.6.cloned.1.call-start
  93.9 102.3 %reduce-scatter.4.cloned.1.call-done = bf16[112,224]{1,0:T(8,128)(2,1)} async-done(((bf16[3584,224]{1,0:T(8,128)(2,1)}), bf16[112,224]{1,0:T(8,128)(2,1)}) %reduce-scatter.4.cloned.1.call-update) | async-done | bytes 50192
  196.3 0.0 all-gather.6.cloned.1.call-update
  196.3 0.0 all-gather.8.cloned.1.call-start
  196.3 0.9 copy.5
  197.3 0.0 copy-start
  197.3 33.4 %all_gather.15 = bf16[3584,112]{1,0:T(8,128)(2,1)S(1)} all-gather(bf16[224,112]{1,0:T(8,128)(2,1)S(1)} %copy.5), channel_id=1, replica_groups=mesh['row'=16,'col'=32] {'row'}, dimensions={0}, use_global_device_ids=true | all-gather | bytes 852992 | tf_op jit(solution)/shard_map/all_gather | solution.py:33
  230.6 27.9 %all-gather.6.cloned.1.call-done = bf16[224,3584]{0,1:T(8,128)(2,1)} async-done(((bf16[224,112]{0,1:T(8,128)(2,1)}), bf16[224,3584]{0,1:T(8,128)(2,1)}) %all-gather.6.cloned.1.call-update) | async-done | bytes 1605648 | tf_op jit(solution)/shard_map/all_gather | solution.py:30
  258.6 2.2 fusion.3
  260.7 0.7 copy.3
  261.5 0.0 all-gather.8.cloned.1.call-update
  261.5 56.6 %all-gather.8.cloned.1.call-done = bf16[224,3584]{0,1:T(8,128)(2,1)} async-done(((bf16[224,112]{0,1:T(8,128)(2,1)}), bf16[224,3584]{0,1:T(8,128)(2,1)}) %all-gather.8.cloned.1.call-update) | async-done | bytes 1605648 | tf_op jit(solution)/shard_map/all_gather | solution.py:37
  318.1 0.0 copy-done
  318.1 5.0 %fusion.1 = bf16[224,576]{1,0:T(8,128)(2,1)} fusion(bf16[224,3584]{0,1:T(8,128)(2,1)} %all-gather.8.cloned.1.call-done, bf16[3584,576]{1,0:T(8,128)(2,1)} %all-gather.4.cloned.1.call-done, bf16[224,576]{1,0:T(8,128)(2,1)S(1)} %copy-done), kind=kOutput, calls=%fused_computation.3 | convolution fusion | flops 925489152 | bytes 6250496 | tf_op jit(solution)/shard_map/dot_general | solution.py:38
Async XLA Ops:
  6.5 80.9 %all-gather.4.cloned.1.call-start = ((), (), s32[]{:S(2)}) async-start(), calls=%async_computation.1 | async-start | bytes 4874240 | tf_op jit(solution)/shard_map/all_gather | solution.py:20
  7.3 189.0 %reduce-scatter.4.cloned.1.call-start = ((), (), s32[]{:S(2)}) async-start(), calls=%async_computation.4 | async-start | bytes 1892352
  93.9 164.7 %all-gather.6.cloned.1.call-start = ((), (), s32[]{:S(2)}) async-start(), calls=%async_computation.2 | async-start | bytes 1892352 | tf_op jit(solution)/shard_map/all_gather | solution.py:30
  196.3 121.8 %all-gather.8.cloned.1.call-start = ((), (), s32[]{:S(2)}) async-start(), calls=%async_computation.3 | async-start | bytes 1892352 | tf_op jit(solution)/shard_map/all_gather | solution.py:37
  197.3 120.8 %copy-start = (bf16[224,576]{1,0:T(8,128)(2,1)S(1)}, bf16[224,576]{1,0:T(8,128)(2,1)}, u32[]{:S(2)}) copy-start(bf16[224,576]{1,0:T(8,128)(2,1)} %param.1) | copy-start | bytes 774148
Sparse Core Ops, SparseCore 0:
  9.4 77.9 all-gather.3
  94.0 102.2 reduce-scatter.3
  199.4 59.1 all-gather.5
  261.6 56.4 all-gather.7
where the time goes:
time: 330 us
  waiting for transfers between devices  268 us (81%)
  blocking collectives  33.4 us (10%)
  between operations  13.2 us (4%)
  matrix products  11.3 us (3%)
  local copies, waits for them, and re-layouts  3.96 us (1%)
    unnamed x5, waiting for transfers between devices  103 us
    all_gather x1, waiting for transfers between devices, per_device(): lax.all_gather(iterate, 'row', axis=0, tiled=True)  80.2 us
    all_gather x1, waiting for transfers between devices, per_device(): factor_panel = lax.all_gather(factor, 'col', axis=1, tiled=True)  56.6 us
    all_gather x1, blocking collectives, per_device(): lax.all_gather(gram_tile, 'row', axis=0, tiled=True)  33.4 us
    all_gather x1, waiting for transfers between devices, per_device(): gram_panel = lax.all_gather(gram_tile, 'col', axis=1, tiled=True)  27.9 us
  transfers between devices with their start and end apart: 4, of which 4 were waited for; matrix products, arithmetic and copies ran while one was open for 0% of the time, Pallas kernels for 0%

commit v1 on v0

v1 whole, which is shorter than its diff:
```python
import math

import jax
import jax.numpy as jnp
from jax import lax
from jax.experimental import pallas as pl
from jax.experimental.pallas import tpu as pltpu
from jax.sharding import PartitionSpec as P

MESH = pl.DeviceIdType.MESH
coef_a = 3.4445
coef_b = -4.775
coef_c = 2.0315

Z, X, YH = 8, 4, 4
N_ROW = 2 * Z

X_AT = 0
CORE_AT = X_AT + 15
XR_AT = CORE_AT + 16
YR_AT = XR_AT + 16
A_AT = YR_AT + 3
B_AT = A_AT + 16
BC_AT = B_AT + 15
F_AT = BC_AT + 16
FC_AT = F_AT + 16
N_SEM = FC_AT + 16

KIND = {
    "f1": (0, -1), "f2": (0, -2), "f3": (0, -3), "f4": (0, -4),
    "b1": (0, 1), "b2": (0, 2), "b3": (0, 3),
    "o1": (1, -1), "o2": (1, -2), "o3": (1, -3),
    "y0": (1, 0), "y1": (1, 1), "y2": (1, 2), "y3": (1, 3), "y4": (1, 4),
}
NUMBER = {name: i for i, name in enumerate(KIND)}
STAGES = (
    (("f1", (("f", "f2"),)), ("b1", (("b", "b2"), ("y", "y1"))), ("y0", (("f", "o1"),))),
    (("f2", (("f", "f3"),)), ("b2", (("b", "b3"), ("y", "y2"))), ("o1", (("f", "o2"),)), ("y1", ())),
    (("f3", (("f", "f4"),)), ("b3", (("y", "y3"),)), ("o2", (("f", "o3"),)), ("y2", ())),
    (("f4", (("y", "y4"),)), ("o3", ()), ("y3", ())),
    (("y4", ()),),
)


def kernel(
    scale, x_ref, o_ref, xbuf, pbuf, cbuf, ysum, xrecv, ysend, yrecv, abuf, bbuf, fbuf, acc, send_sem, recv_sem
):
    rows, half = x_ref.shape[0], x_ref.shape[0] // 2
    r, c = lax.axis_index("row"), lax.axis_index("col")
    yl, z = r // Z, lax.rem(r, Z)
    x, yh, k = c // (2 * YH), lax.rem(c // 2, YH), lax.rem(c, 2)
    me = c // 2
    e = 1 - 2 * k
    mine = pl.ds(pl.multiple_of(k * half, half), half)
    other = pl.ds(pl.multiple_of((1 - k) * half, half), half)

    def at_row(side, steps):
        return lax.rem(yl + side, 2) * Z + lax.rem(z + steps * e + 2 * Z, Z)

    def at_col(dx, dy, dk=0):
        return lax.rem(x + dx, X) * (2 * YH) + lax.rem(yh + dy, YH) * 2 + lax.rem(k + dk, 2)

    link = {"f": (at_row(0, 1), c), "b": (at_row(0, -1), c), "y": (at_row(1, 0), c)}
    sibling = (r, at_col(0, 0, 1))

    barrier = pltpu.get_barrier_semaphore()
    partners = [*link.values(), sibling]
    partners += [(r, at_col(i, 0)) for i in range(1, X)] + [(r, at_col(0, j)) for j in range(1, YH)]
    for partner in partners:
        pl.semaphore_signal(barrier, inc=1, device_id=partner, device_id_type=MESH)
    pl.semaphore_wait(barrier, len(partners))

    def copy(src, dst, sent, received, device):
        return pltpu.make_async_remote_copy(
            src_ref=src, dst_ref=dst, send_sem=send_sem.at[sent], recv_sem=recv_sem.at[received],
            device_id=device, device_id_type=MESH,
        )

    def arrived(dst, received):
        copy(dst, dst, received, received, sibling).wait_recv()

    def left(src, sent):
        copy(src, src, sent, sent, sibling).wait_send()

    def x_send(src, at, name, s):
        number = X_AT + NUMBER[name]
        copy(src, xbuf.at[s], number, number, link[at]).start()

    for at, name in (("f", "f1"), ("b", "b1"), ("y", "y0")):
        x_send(x_ref, at, name, r)
    xbuf[r] = x_ref[...]

    def gram(s):
        product = lax.dot_general(
            x_ref[...], xbuf[s], (((1,), (1,)), ((), ())), preferred_element_type=jnp.float32
        )
        pbuf[s] = product.astype(jnp.bfloat16)
        copy(pbuf.at[s, other], cbuf.at[s], CORE_AT + s, CORE_AT + s, sibling).start()

    def reduce_x(s):
        arrived(cbuf.at[s], CORE_AT + s)
        total = pbuf[s, mine].astype(jnp.float32) + cbuf[s].astype(jnp.float32)
        ysum[s] = total.astype(jnp.bfloat16)
        to, place = s // YH, lax.rem(s, YH)
        apart = lax.rem(x - to + X, X)

        @pl.when(apart != 0)
        def _():
            copy(
                ysum.at[s], xrecv.at[apart, place], XR_AT + s, XR_AT + apart * YH + place,
                (r, to * (2 * YH) + yh * 2 + k),
            ).start()

    gram(r)
    pending = [r]
    for stage in STAGES:
        todo = []
        for name, onward in stage:
            s = at_row(*KIND[name])
            arrived(xbuf.at[s], X_AT + NUMBER[name])
            for at, new in onward:
                x_send(xbuf.at[s], at, new, s)
            todo.append(s)
        for s in pending:
            reduce_x(s)
        for s in todo:
            gram(s)
        pending = todo
    for s in pending:
        reduce_x(s)

    own = None
    for j in (1, 2, 3, 0):
        place = lax.rem(yh + j, YH)
        total = ysum[x * YH + place].astype(jnp.float32)
        for i in range(1, X):
            arrived(xrecv.at[i, place], XR_AT + i * YH + place)
            total = total + xrecv[i, place].astype(jnp.float32)
        if j:
            ysend[j - 1] = total.astype(jnp.bfloat16)
            copy(
                ysend.at[j - 1], yrecv.at[j - 1], YR_AT + j - 1, YR_AT + j - 1, (r, at_col(0, j))
            ).start()
        else:
            own = total
    for j in range(1, YH):
        arrived(yrecv.at[j - 1], YR_AT + j - 1)
        own = own + yrecv[j - 1].astype(jnp.float32)
    tile = own.astype(jnp.bfloat16)
    abuf[me] = tile
    bbuf[r, mine] = tile

    def b_send(src, at, name, s):
        number = B_AT + NUMBER[name]
        copy(src, bbuf.at[s, mine], number, number, link[at]).start()

    def b_share(s):
        copy(bbuf.at[s, mine], bbuf.at[s, mine], BC_AT + s, BC_AT + s, sibling).start()

    def a_spread(s, first):
        for i in range(1, X):
            copy(abuf.at[s], abuf.at[s], A_AT + first + i, A_AT + s, (r, at_col(i, 0))).start()

    for at, name in (("f", "f1"), ("b", "b1"), ("y", "y0")):
        b_send(bbuf.at[r, mine], at, name, r)
    for j in range(1, YH):
        copy(abuf.at[me], abuf.at[me], A_AT + j - 1, A_AT + me, (r, at_col(0, j))).start()
    a_spread(me, 2)
    b_share(r)
    for index, stage in enumerate(STAGES):
        for name, onward in stage:
            s = at_row(*KIND[name])
            arrived(bbuf.at[s, mine], B_AT + NUMBER[name])
            for at, new in onward:
                b_send(bbuf.at[s, mine], at, new, s)
            b_share(s)
        j = index + 1
        if j < YH:
            s = x * YH + lax.rem(yh + YH - j, YH)
            arrived(abuf.at[s], A_AT + s)
            a_spread(s, 2 + 3 * j)
    for i in range(1, X):
        for j in range(YH):
            s = lax.rem(x + i, X) * YH + lax.rem(yh + j, YH)
            arrived(abuf.at[s], A_AT + s)

    def wait_shared(s, _):
        arrived(bbuf.at[s, other], BC_AT + s)
        return 0

    lax.fori_loop(0, N_ROW, wait_shared, 0)

    def square(s, total):
        return total + jnp.dot(abuf[s], bbuf[s], preferred_element_type=jnp.float32)

    squared = lax.fori_loop(0, N_ROW, square, jnp.zeros((half, rows), jnp.float32))
    fbuf[me, mine] = (coef_b * tile.astype(jnp.float32) + coef_c * squared).astype(jnp.bfloat16)

    def f_share(s):
        copy(fbuf.at[s, mine], fbuf.at[s, mine], FC_AT + s, FC_AT + s, sibling).start()

    def f_spread(s, first):
        for i in range(1, X):
            copy(
                fbuf.at[s, mine], fbuf.at[s, mine], F_AT + first + i, F_AT + s, (r, at_col(i, 0))
            ).start()

    for j in range(1, YH):
        copy(fbuf.at[me, mine], fbuf.at[me, mine], F_AT + j - 1, F_AT + me, (r, at_col(0, j))).start()
    f_spread(me, 2)
    f_share(me)
    acc[...] = coef_a * x_ref[...].astype(jnp.float32)
    for j in range(1, YH):
        s = x * YH + lax.rem(yh + YH - j, YH)
        arrived(fbuf.at[s, mine], F_AT + s)
        f_spread(s, 2 + 3 * j)
        f_share(s)
    for i in range(1, X):
        for j in range(YH):
            s = lax.rem(x + i, X) * YH + lax.rem(yh + j, YH)
            arrived(fbuf.at[s, mine], F_AT + s)
            f_share(s)

    def apply(j, carry):
        s = lax.rem(me + j, N_ROW)
        arrived(fbuf.at[s, other], FC_AT + s)
        acc[...] += jnp.dot(fbuf[s], xbuf[s], preferred_element_type=jnp.float32)
        return carry

    lax.fori_loop(0, N_ROW, apply, 0)
    o_ref[...] = (scale * acc[...]).astype(o_ref.dtype)

    for number in range(15):
        left(x_ref, X_AT + number)
        left(abuf.at[0], A_AT + number)
        left(abuf.at[0], B_AT + number)
        left(abuf.at[0], F_AT + number)
    for j in range(YH - 1):
        left(ysend.at[j], YR_AT + j)

    def all_left(s, carry):
        left(cbuf.at[s], CORE_AT + s)
        left(cbuf.at[s], BC_AT + s)
        left(cbuf.at[s], FC_AT + s)

        @pl.when(s // YH != x)
        def _():
            left(ysum.at[s], XR_AT + s)

        return carry

    lax.fori_loop(0, N_ROW, all_left, 0)


def solution(mesh):
    def step(iterate):
        rows, width = iterate.shape
        half, n = rows // 2, width * mesh.shape["col"]
        bf16 = jnp.bfloat16

        def body(*refs):
            kernel(math.sqrt(n), *refs)

        return pl.pallas_call(
            body,
            out_shape=jax.ShapeDtypeStruct((rows, width), bf16),
            in_specs=[pl.BlockSpec(memory_space=pltpu.VMEM)],
            out_specs=pl.BlockSpec(memory_space=pltpu.VMEM),
            scratch_shapes=[
                pltpu.VMEM((N_ROW, rows, width), bf16),
                pltpu.VMEM((N_ROW, rows, rows), bf16),
                pltpu.VMEM((N_ROW, half, rows), bf16),
                pltpu.VMEM((N_ROW, half, rows), bf16),
                pltpu.VMEM((X, YH, half, rows), bf16),
                pltpu.VMEM((YH - 1, half, rows), bf16),
                pltpu.VMEM((YH - 1, half, rows), bf16),
                pltpu.VMEM((N_ROW, half, rows), bf16),
                pltpu.VMEM((N_ROW, rows, rows), bf16),
                pltpu.VMEM((N_ROW, rows, rows), bf16),
                pltpu.VMEM((rows, width), jnp.float32),
                pltpu.SemaphoreType.DMA((N_SEM,)),
                pltpu.SemaphoreType.DMA((N_SEM,)),
            ],
            compiler_params=pltpu.CompilerParams(
                collective_id=0, has_side_effects=True, vmem_limit_bytes=48 << 20
            ),
            cost_estimate=pl.CostEstimate(
                flops=2 * rows * N_ROW * rows * (2 * width + half), bytes_accessed=4 * rows * width, transcendentals=0
            ),
        )(iterate)

    return jax.shard_map(
        step, mesh=mesh, in_specs=(P("row", "col"),), out_specs=P("row", "col"), check_vma=False
    )
```

time: 330 us -> 114 us (0.35)
  waiting for transfers between devices: 268 us -> 0 us
  Pallas kernels: 0 us -> 110 us
  blocking collectives: 33.4 us -> 0 us
  between operations: 13.2 us -> 0.01 us
  matrix products: 11.3 us -> 0 us
    all_gather x3 -> x0, waiting for transfers between devices: 165 us -> none  [the longest x1 80.2 us: per_device(): lax.all_gather(iterate, 'row', axis=0, tiled=True)]
    pallas_call x0 -> x1, Pallas kernels: none -> 110 us  [step(): pl.pallas_call(body, out_shape=jax.ShapeDtypeStruct((rows, width), bf16),...]
    unnamed x5 -> x0, waiting for transfers between devices: 103 us -> none
    all_gather x1 -> x0, blocking collectives: 33.4 us -> none  [per_device(): lax.all_gather(gram_tile, 'row', axis=0, tiled=True)]
    dot_general x3 -> x0, matrix products: 11.3 us -> none  [the longest x1 5.02 us: per_device(): jnp.dot(factor_panel, lax.all_gather(iterate, 'row', axis=0, tiled=True),...]
  transfers between devices with their start and end apart: 4 -> 0, of which waited for: 4 -> 0; matrix products, arithmetic and copies ran while one was open for 0% -> 0% of each run, Pallas kernels for 0% -> 0%
where the time goes in v1:
time: 114 us; the launch traced here: 112 us
  Pallas kernels  110 us (96%)
  local copies, waits for them, and re-layouts  1.67 us (1%)
    pallas_call x1, Pallas kernels, step(): pl.pallas_call(body, out_shape=jax.ShapeDtypeStruct((rows, width), bf16),...  110 us

profile of v1, /device:TPU:1, one launch (start us, length us, event | category | flops | bytes accessed | tf_op | source)
XLA Modules:
  0.0 112.0 jit_solution(1799224001774320137)
XLA Ops:
  0.0 0.0 copy-start
  0.0 1.0 copy-done
  1.0 110.3 %shard_map.17 = bf16[224,576]{1,0:T(8,128)(2,1)S(1)} custom-call(bf16[224,576]{1,0:T(8,128)(2,1)S(1)} %copy-done), custom_call_target="tpu_custom_call" | custom-call | flops 2029518848 | bytes 516096 | tf_op jit(solution)/shard_map/pallas_call | solution.py:264
  111.3 0.7 copy.3
Async XLA Ops:
  0.0 1.0 copy-start

commit v2 on v1

--- a/solution.py
+++ b/solution.py
@@ -18,57 +18,95 @@
 X_AT = 0
 CORE_AT = X_AT + 15
 XR_AT = CORE_AT + 16
-YR_AT = XR_AT + 16
-A_AT = YR_AT + 3
+D_AT = XR_AT + 16
+A_AT = D_AT + 4
 B_AT = A_AT + 16
 BC_AT = B_AT + 15
 F_AT = BC_AT + 16
 FC_AT = F_AT + 16
 N_SEM = FC_AT + 16
 
+HERE = (0, 0)
 KIND = {
-    "f1": (0, -1), "f2": (0, -2), "f3": (0, -3), "f4": (0, -4),
-    "b1": (0, 1), "b2": (0, 2), "b3": (0, 3),
-    "o1": (1, -1), "o2": (1, -2), "o3": (1, -3),
-    "y0": (1, 0), "y1": (1, 1), "y2": (1, 2), "y3": (1, 3), "y4": (1, 4),
+    "m1": (0, -1), "m2": (0, -2), "m3": (0, -3), "p1": (0, 1), "p2": (0, 2), "p3": (0, 3), "q4": (0, 4),
+    "y0": (1, 0), "y1": (1, 1), "y2": (1, 2), "y3": (1, 3), "r4": (1, 4), "n1": (1, -1), "n2": (1, -2), "n3": (1, -3),
 }
 NUMBER = {name: i for i, name in enumerate(KIND)}
-STAGES = (
-    (("f1", (("f", "f2"),)), ("b1", (("b", "b2"), ("y", "y1"))), ("y0", (("f", "o1"),))),
-    (("f2", (("f", "f3"),)), ("b2", (("b", "b3"), ("y", "y2"))), ("o1", (("f", "o2"),)), ("y1", ())),
-    (("f3", (("f", "f4"),)), ("b3", (("y", "y3"),)), ("o2", (("f", "o3"),)), ("y2", ())),
-    (("f4", (("y", "y4"),)), ("o3", ()), ("y3", ())),
-    (("y4", ()),),
+ONWARD = {
+    "m1": (("u", "m2"),), "m2": (("u", "m3"),), "m3": (("y", "n3"),),
+    "p1": (("d", "p2"), ("y", "y1")), "p2": (("d", "p3"), ("y", "y2")), "p3": (("d", "q4"), ("y", "y3")),
+    "y0": (("u", "n1"),), "n1": (("u", "n2"),), "y3": (("d", "r4"),),
+}
+STAGES = (("m1", "p1", "y0"), ("m2", "p2", "y1", "n1"), ("m3", "p3", "y2", "n2"), ("q4", "y3", "n3"), ("r4",))
+T1, T2 = (1, 1), (1, 2)
+BLOCKS = (
+    (HERE, HERE), ((0, 1), (0, -1)), ((0, -1), (0, 2)), ((0, -2), T2),
+    (HERE, (0, 1)), (HERE, (1, 0)), ((0, 2), (0, -1)), (HERE, T1),
+    ((0, 1), HERE), ((0, -2), (0, 2)), (T1, HERE), ((0, -1), T1),
+    ((0, -1), (0, 1)), (T1, (0, -1)), ((0, -2), T1), (T1, (0, -2)),
 )
+FIRST = (0, 4, 8, 12, 1, 5)
+SECOND = (2, 6, 9, 7, 10, 11, 13, 14, 15)
+LAST = (3,)
+
+
+def pick(index, values):
+    n = len(values)
+    return sum(((n - lax.rem(index - i + n, n)) // n) * value for i, value in enumerate(values) if value)
 
 
 def kernel(
-    scale, x_ref, o_ref, xbuf, pbuf, cbuf, ysum, xrecv, ysend, yrecv, abuf, bbuf, fbuf, acc, send_sem, recv_sem
+    scale, x_ref, o_ref, xbuf, pbuf, cbuf, xsum, xrecv, dsend, drecv, abuf, bbuf, fbuf, acc, send_sem, recv_sem
 ):
     rows, half = x_ref.shape[0], x_ref.shape[0] // 2
     r, c = lax.axis_index("row"), lax.axis_index("col")
     yl, z = r // Z, lax.rem(r, Z)
     x, yh, k = c // (2 * YH), lax.rem(c // 2, YH), lax.rem(c, 2)
     me = c // 2
-    e = 1 - 2 * k
     mine = pl.ds(pl.multiple_of(k * half, half), half)
     other = pl.ds(pl.multiple_of((1 - k) * half, half), half)
 
     def at_row(side, steps):
-        return lax.rem(yl + side, 2) * Z + lax.rem(z + steps * e + 2 * Z, Z)
+        return lax.rem(yl + side, 2) * Z + lax.rem(z + steps + Z, Z)
 
     def at_col(dx, dy, dk=0):
         return lax.rem(x + dx, X) * (2 * YH) + lax.rem(yh + dy, YH) * 2 + lax.rem(k + dk, 2)
 
-    link = {"f": (at_row(0, 1), c), "b": (at_row(0, -1), c), "y": (at_row(1, 0), c)}
+    link = {"u": (at_row(0, 1), c), "d": (at_row(0, -1), c), "y": (at_row(1, 0), c)}
     sibling = (r, at_col(0, 0, 1))
+
+    owner, at_home = [], []
+    for place in range(YH):
+        column = [BLOCKS[i * YH + place] for i in range(X)]
+        to_row = at_row(pick(x, [a[0] for a, b in column]), pick(x, [a[1] for a, b in column]))
+        to = at_row(pick(x, [b[0] for a, b in column]), pick(x, [b[1] for a, b in column]))
+        owner.append((to_row, to * 2 + k))
+        at_home.append(jnp.logical_and(to_row == r, to == me))
+    apart = {((b[0] - a[0]) % 2, (b[1] - a[1]) % Z): (n, a) for n, (a, b) in enumerate(BLOCKS)}
+    found = [apart[side, steps] for side in range(2) for steps in range(Z)]
+    from_me = lax.rem(me // Z - yl + 2, 2) * Z + lax.rem(lax.rem(me, Z) - z + Z, Z)
+    from_x = pick(from_me, [n // YH for n, a in found])
+    from_row = at_row(pick(from_me, [a[0] for n, a in found]), 0 - pick(from_me, [a[1] for n, a in found]))
+    from_home = jnp.logical_and(from_row == r, from_x == x)
 
     barrier = pltpu.get_barrier_semaphore()
     partners = [*link.values(), sibling]
     partners += [(r, at_col(i, 0)) for i in range(1, X)] + [(r, at_col(0, j)) for j in range(1, YH)]
     for partner in partners:
         pl.semaphore_signal(barrier, inc=1, device_id=partner, device_id_type=MESH)
-    pl.semaphore_wait(barrier, len(partners))
+    for j in range(YH):
+        there = lax.rem(yh + j, YH)
+
+        def greet():
+            pl.semaphore_signal(
+                barrier, inc=1, device_id=(from_row, from_x * (2 * YH) + there * 2 + k), device_id_type=MESH
+            )
+
+        if j:
+            greet()
+        else:
+            pl.when(jnp.logical_not(from_home))(greet)
+    pl.semaphore_wait(barrier, len(partners) + YH - from_home.astype(jnp.int32))
 
     def copy(src, dst, sent, received, device):
         return pltpu.make_async_remote_copy(
@@ -86,66 +124,97 @@
         number = X_AT + NUMBER[name]
         copy(src, xbuf.at[s], number, number, link[at]).start()
 
-    for at, name in (("f", "f1"), ("b", "b1"), ("y", "y0")):
+    def x_wait(name):
+        s = at_row(*KIND[name])
+        arrived(xbuf.at[s], X_AT + NUMBER[name])
+
+    def x_onward(name):
+        s = at_row(*KIND[name])
+        for at, new in ONWARD.get(name, ()):
+            x_send(xbuf.at[s], at, new, s)
+
+    def x_pass(*names):
+        for name in names:
+            x_wait(name)
+            x_onward(name)
+
+    for at, name in (("u", "m1"), ("d", "p1"), ("y", "y0")):
         x_send(x_ref, at, name, r)
     xbuf[r] = x_ref[...]
 
-    def gram(s):
+    def gram(n):
+        a, b = BLOCKS[n]
         product = lax.dot_general(
-            x_ref[...], xbuf[s], (((1,), (1,)), ((), ())), preferred_element_type=jnp.float32
+            xbuf[at_row(*a)], xbuf[at_row(*b)], (((1,), (1,)), ((), ())), preferred_element_type=jnp.float32
         )
-        pbuf[s] = product.astype(jnp.bfloat16)
-        copy(pbuf.at[s, other], cbuf.at[s], CORE_AT + s, CORE_AT + s, sibling).start()
-
-    def reduce_x(s):
-        arrived(cbuf.at[s], CORE_AT + s)
-        total = pbuf[s, mine].astype(jnp.float32) + cbuf[s].astype(jnp.float32)
-        ysum[s] = total.astype(jnp.bfloat16)
-        to, place = s // YH, lax.rem(s, YH)
+        pbuf[n] = product.astype(jnp.bfloat16)
+        copy(pbuf.at[n, other], cbuf.at[n], CORE_AT + n, CORE_AT + n, sibling).start()
+
+    def reduce_x(n):
+        arrived(cbuf.at[n], CORE_AT + n)
+        total = pbuf[n, mine].astype(jnp.float32) + cbuf[n].astype(jnp.float32)
+        xsum[n] = total.astype(jnp.bfloat16)
+        to, place = n // YH, n % YH
         apart = lax.rem(x - to + X, X)
 
         @pl.when(apart != 0)
         def _():
             copy(
-                ysum.at[s], xrecv.at[apart, place], XR_AT + s, XR_AT + apart * YH + place,
+                xsum.at[n], xrecv.at[apart, place], XR_AT + n, XR_AT + apart * YH + place,
                 (r, to * (2 * YH) + yh * 2 + k),
             ).start()
 
-    gram(r)
-    pending = [r]
-    for stage in STAGES:
-        todo = []
-        for name, onward in stage:
-            s = at_row(*KIND[name])
-            arrived(xbuf.at[s], X_AT + NUMBER[name])
-            for at, new in onward:
-                x_send(xbuf.at[s], at, new, s)
-            todo.append(s)
-        for s in pending:
-            reduce_x(s)
-        for s in todo:
-            gram(s)
-        pending = todo
-    for s in pending:
-        reduce_x(s)
-
-    own = None
-    for j in (1, 2, 3, 0):
-        place = lax.rem(yh + j, YH)
-        total = ysum[x * YH + place].astype(jnp.float32)
+    def deliver(place):
+        total = xsum[x * YH + place].astype(jnp.float32)
         for i in range(1, X):
             arrived(xrecv.at[i, place], XR_AT + i * YH + place)
             total = total + xrecv[i, place].astype(jnp.float32)
-        if j:
-            ysend[j - 1] = total.astype(jnp.bfloat16)
-            copy(
-                ysend.at[j - 1], yrecv.at[j - 1], YR_AT + j - 1, YR_AT + j - 1, (r, at_col(0, j))
-            ).start()
-        else:
-            own = total
+        dsend[place] = total.astype(jnp.bfloat16)
+
+        @pl.when(jnp.logical_not(at_home[place]))
+        def _():
+            copy(dsend.at[place], drecv.at[yh], D_AT + place, D_AT + yh, owner[place]).start()
+
+        @pl.when(at_home[place])
+        def _():
+            drecv[yh] = dsend[place]
+
+    gram(FIRST[0])
+    x_wait("m1")
+    x_onward("m1")
+    x_wait("p1")
+    x_onward("p1")
+    x_wait("y0")
+    for n in FIRST[1:]:
+        gram(n)
+    for n in FIRST:
+        reduce_x(n)
+    x_pass("m2", "p2")
+    x_onward("y0")
+    x_wait("y1")
+    for n in SECOND:
+        gram(n)
+    for n in SECOND:
+        reduce_x(n)
+    x_wait("y2")
+    for n in LAST:
+        gram(n)
+    x_pass("p3")
+    for n in LAST:
+        reduce_x(n)
+    for place in range(YH):
+        deliver(place)
+    x_pass("m3", "n1")
+
+    @pl.when(jnp.logical_not(from_home))
+    def _():
+        arrived(drecv.at[yh], D_AT + yh)
+
+    own = drecv[yh].astype(jnp.float32)
     for j in range(1, YH):
-        arrived(yrecv.at[j - 1], YR_AT + j - 1)
-        own = own + yrecv[j - 1].astype(jnp.float32)
+        there = lax.rem(yh + j, YH)
+        arrived(drecv.at[there], D_AT + there)
+        own = own + drecv[there].astype(jnp.float32)
     tile = own.astype(jnp.bfloat16)
     abuf[me] = tile
     bbuf[r, mine] = tile
@@ -161,17 +230,18 @@
         for i in range(1, X):
             copy(abuf.at[s], abuf.at[s], A_AT + first + i, A_AT + s, (r, at_col(i, 0))).start()
 
-    for at, name in (("f", "f1"), ("b", "b1"), ("y", "y0")):
+    for at, name in (("u", "m1"), ("d", "p1"), ("y", "y0")):
         b_send(bbuf.at[r, mine], at, name, r)
     for j in range(1, YH):
         copy(abuf.at[me], abuf.at[me], A_AT + j - 1, A_AT + me, (r, at_col(0, j))).start()
     a_spread(me, 2)
     b_share(r)
+    x_pass("y3")
     for index, stage in enumerate(STAGES):
-        for name, onward in stage:
+        for name in stage:
             s = at_row(*KIND[name])
             arrived(bbuf.at[s, mine], B_AT + NUMBER[name])
-            for at, new in onward:
+            for at, new in ONWARD.get(name, ()):
                 b_send(bbuf.at[s, mine], at, new, s)
             b_share(s)
         j = index + 1
@@ -221,6 +291,9 @@
             arrived(fbuf.at[s, mine], F_AT + s)
             f_share(s)
 
+    for name in ("q4", "n2", "n3", "r4"):
+        x_wait(name)
+
     def apply(j, carry):
         s = lax.rem(me + j, N_ROW)
         arrived(fbuf.at[s, other], FC_AT + s)
@@ -235,8 +308,12 @@
         left(abuf.at[0], A_AT + number)
         left(abuf.at[0], B_AT + number)
         left(abuf.at[0], F_AT + number)
-    for j in range(YH - 1):
-        left(ysend.at[j], YR_AT + j)
+    for place in range(YH):
+
+        @pl.when(jnp.logical_not(at_home[place]))
+        def _():
+            left(dsend.at[place], D_AT + place)
+
 
     def all_left(s, carry):
         left(cbuf.at[s], CORE_AT + s)
@@ -245,7 +322,7 @@
 
         @pl.when(s // YH != x)
         def _():
-            left(ysum.at[s], XR_AT + s)
+            left(xsum.at[s], XR_AT + s)
 
         return carry
 
@@ -272,8 +349,8 @@
                 pltpu.VMEM((N_ROW, half, rows), bf16),
                 pltpu.VMEM((N_ROW, half, rows), bf16),
                 pltpu.VMEM((X, YH, half, rows), bf16),
-                pltpu.VMEM((YH - 1, half, rows), bf16),
-                pltpu.VMEM((YH - 1, half, rows), bf16),
+                pltpu.VMEM((YH, half, rows), bf16),
+                pltpu.VMEM((YH, half, rows), bf16),
                 pltpu.VMEM((N_ROW, half, rows), bf16),
                 pltpu.VMEM((N_ROW, rows, rows), bf16),
                 pltpu.VMEM((N_ROW, rows, rows), bf16),

time: 114 us -> 103 us (0.904); the launches traced: 112 us -> 103 us
  Pallas kernels: 110 us -> 101 us
    pallas_call x1, Pallas kernels: 110 us -> 101 us  [step(): pl.pallas_call(body, out_shape=jax.ShapeDtypeStruct((rows, width), bf16),...]
where the time goes in v2:
time: 103 us
  Pallas kernels  101 us (98%)
  local copies, waits for them, and re-layouts  1.67 us (2%)
    pallas_call x1, Pallas kernels, step(): pl.pallas_call(body, out_shape=jax.ShapeDtypeStruct((rows, width), bf16),...  101 us

profile of v2, /device:TPU:1, one launch (start us, length us, event | category | flops | bytes accessed | tf_op | source)
XLA Modules:
  0.0 103.0 jit_solution(10841141687240979173)
XLA Ops:
  0.0 0.0 copy-start
  0.0 1.0 copy-done
  1.0 101.3 %shard_map.17 = bf16[224,576]{1,0:T(8,128)(2,1)S(1)} custom-call(bf16[224,576]{1,0:T(8,128)(2,1)S(1)} %copy-done), custom_call_target="tpu_custom_call" | custom-call | flops 2029518848 | bytes 516096 | tf_op jit(solution)/shard_map/pallas_call | solution.py:341
  102.3 0.7 copy.3
Async XLA Ops:
  0.0 1.0 copy-start

commit v3 on v2

v3 whole, which is shorter than its diff:
```python
import math

import jax
import jax.numpy as jnp
from jax import lax
from jax.experimental import pallas as pl
from jax.experimental.pallas import tpu as pltpu
from jax.sharding import PartitionSpec as P

MESH = pl.DeviceIdType.MESH
coef_a = 3.4445
coef_b = -4.775
coef_c = 2.0315

Z, X, YH = 8, 4, 4
N_ROW = 2 * Z

X_AT = 0
CORE_AT = X_AT + 15
XR_AT = CORE_AT + 16
Y_AT = XR_AT + 16
G_AT = Y_AT + 4
A_AT = G_AT + 1
B_AT = A_AT + 16
BC_AT = B_AT + 15
F_AT = BC_AT + 16
FC_AT = F_AT + 16
N_SEM = FC_AT + 16

HERE = (0, 0)
KIND = {
    "m1": (0, -1), "m2": (0, -2), "m3": (0, -3), "p1": (0, 1), "p2": (0, 2), "p3": (0, 3), "q4": (0, 4),
    "y0": (1, 0), "y1": (1, 1), "y2": (1, 2), "y3": (1, 3), "r4": (1, 4), "n1": (1, -1), "n2": (1, -2), "n3": (1, -3),
}
NUMBER = {name: i for i, name in enumerate(KIND)}
ONWARD = {
    "m1": (("u", "m2"),), "m2": (("u", "m3"),), "m3": (("y", "n3"),),
    "p1": (("d", "p2"), ("y", "y1")), "p2": (("d", "p3"), ("y", "y2")), "p3": (("d", "q4"), ("y", "y3")),
    "y0": (("u", "n1"),), "n1": (("u", "n2"),), "y3": (("d", "r4"),),
}
PANEL = {
    "m1": (("y", 0, "n1"),), "p1": (("y", 0, "y1"),),
    "m2": (("z", 1, "m3"), ("y", 0, "n2")), "p2": (("z", -1, "p3"), ("z", -2, "q4"), ("y", 0, "y2")),
    "m3": (("y", 0, "n3"),), "p3": (("y", 0, "y3"),), "q4": (("y", 0, "r4"),),
}
T0, T1, T2 = (1, 0), (1, 1), (1, 2)
BLOCKS = (
    (HERE, HERE), ((0, -1), (0, 2)), ((0, 1), (0, -1)), (T1, (0, -1)),
    (HERE, (0, 1)), ((0, 2), (0, -1)), (T0, HERE), ((0, -2), T1),
    (HERE, (0, -1)), ((0, -2), (0, 2)), ((0, -1), T0), (T1, (0, -2)),
    ((0, -1), (0, 1)), ((0, -1), T1), ((0, 1), T0), ((0, -2), T2),
)
FIRST = (0, 2, 4, 6, 8, 10, 12, 14)
SECOND = (1, 3, 5, 7, 9, 11, 13)
LAST = (15,)


def pick(index, values):
    n = len(values)
    return sum(((n - lax.rem(index - i + n, n)) // n) * value for i, value in enumerate(values) if value)


def kernel(
    scale, x_ref, o_ref, xbuf, pbuf, cbuf, xsum, xrecv, ysend, yrecv, gsend, gtile, abuf, bbuf, fbuf, acc, send_sem, recv_sem
):
    rows, half = x_ref.shape[0], x_ref.shape[0] // 2
    r, c = lax.axis_index("row"), lax.axis_index("col")
    yl, z = r // Z, lax.rem(r, Z)
    x, yh, k = c // (2 * YH), lax.rem(c // 2, YH), lax.rem(c, 2)
    me = yh * X + x
    mine = pl.ds(pl.multiple_of(k * half, half), half)
    other = pl.ds(pl.multiple_of((1 - k) * half, half), half)

    def at_row(side, steps):
        return lax.rem(yl + side, 2) * Z + lax.rem(z + steps + Z, Z)

    def at_col(dx, dy, dk=0):
        return lax.rem(x + dx, X) * (2 * YH) + lax.rem(yh + dy, YH) * 2 + lax.rem(k + dk, 2)

    link = {"u": (at_row(0, 1), c), "d": (at_row(0, -1), c), "y": (at_row(1, 0), c)}
    sibling = (r, at_col(0, 0, 1))

    def block_at(number):
        return at_row(pick(number, [a[0] for a, b in BLOCKS]), pick(number, [a[1] for a, b in BLOCKS])), at_row(
            pick(number, [b[0] for a, b in BLOCKS]), pick(number, [b[1] for a, b in BLOCKS])
        )

    def column(s):
        return lax.rem(s, X) * (2 * YH) + s // X * 2 + k

    to_row, to = block_at(x * YH + yh)
    owner = (to_row, column(to))
    apart = {((b[0] - a[0]) % 2, (b[1] - a[1]) % Z): (n, a) for n, (a, b) in enumerate(BLOCKS)}
    found = [apart[side, steps] for side in range(2) for steps in range(Z)]
    from_me = lax.rem(me // Z - yl + 2, 2) * Z + lax.rem(lax.rem(me, Z) - z + Z, Z)
    from_row = at_row(pick(from_me, [a[0] for n, a in found]), 0 - pick(from_me, [a[1] for n, a in found]))
    source = (from_row, pick(from_me, [n for n, a in found]) * 2 + k)
    at_home = jnp.logical_and(to_row == r, to == me)

    barrier = pltpu.get_barrier_semaphore()
    partners = [*link.values(), sibling]
    partners += [(r, at_col(i, 0)) for i in range(1, X)] + [(r, at_col(0, j)) for j in range(1, YH)]
    for partner in partners:
        pl.semaphore_signal(barrier, inc=1, device_id=partner, device_id_type=MESH)

    @pl.when(jnp.logical_not(at_home))
    def _():
        pl.semaphore_signal(barrier, inc=1, device_id=source, device_id_type=MESH)

    pl.semaphore_wait(barrier, len(partners) + 1 - at_home.astype(jnp.int32))

    def copy(src, dst, sent, received, device):
        return pltpu.make_async_remote_copy(
            src_ref=src, dst_ref=dst, send_sem=send_sem.at[sent], recv_sem=recv_sem.at[received],
            device_id=device, device_id_type=MESH,
        )

    def arrived(dst, received):
        copy(dst, dst, received, received, sibling).wait_recv()

    def left(src, sent):
        copy(src, src, sent, sent, sibling).wait_send()

    def x_send(src, at, name, s):
        number = X_AT + NUMBER[name]
        copy(src, xbuf.at[s], number, number, link[at]).start()

    def x_wait(name):
        s = at_row(*KIND[name])
        arrived(xbuf.at[s], X_AT + NUMBER[name])

    def x_onward(name):
        s = at_row(*KIND[name])
        for at, new in ONWARD.get(name, ()):
            x_send(xbuf.at[s], at, new, s)

    def x_pass(*names):
        for name in names:
            x_wait(name)
            x_onward(name)

    for at, name in (("u", "m1"), ("d", "p1"), ("y", "y0")):
        x_send(x_ref, at, name, r)
    xbuf[r] = x_ref[...]

    def gram(n):
        a, b = BLOCKS[n]
        product = lax.dot_general(
            xbuf[at_row(*a)], xbuf[at_row(*b)], (((1,), (1,)), ((), ())), preferred_element_type=jnp.float32
        )
        pbuf[n] = product.astype(jnp.bfloat16)
        copy(pbuf.at[n, other], cbuf.at[n], CORE_AT + n, CORE_AT + n, sibling).start()

    def reduce_x(n):
        arrived(cbuf.at[n], CORE_AT + n)
        total = pbuf[n, mine].astype(jnp.float32) + cbuf[n].astype(jnp.float32)
        xsum[n] = total.astype(jnp.bfloat16)
        to, place = n // YH, n % YH
        apart = lax.rem(x - to + X, X)

        @pl.when(apart != 0)
        def _():
            copy(
                xsum.at[n], xrecv.at[apart, place], XR_AT + n, XR_AT + apart * YH + place,
                (r, to * (2 * YH) + yh * 2 + k),
            ).start()

    def reduce_y(place):
        total = xsum[x * YH + place].astype(jnp.float32)
        for i in range(1, X):
            arrived(xrecv.at[i, place], XR_AT + i * YH + place)
            total = total + xrecv[i, place].astype(jnp.float32)
        ysend[place] = total.astype(jnp.bfloat16)
        apart = lax.rem(yh - place + YH, YH)

        @pl.when(apart != 0)
        def _():
            copy(
                ysend.at[place], yrecv.at[apart], Y_AT + place, Y_AT + apart,
                (r, x * (2 * YH) + place * 2 + k),
            ).start()

    def deliver():
        total = ysend[yh].astype(jnp.float32)
        for j in range(1, YH):
            arrived(yrecv.at[j], Y_AT + j)
            total = total + yrecv[j].astype(jnp.float32)
        gsend[...] = total.astype(jnp.bfloat16)

        @pl.when(jnp.logical_not(at_home))
        def _():
            copy(gsend, gtile, G_AT, G_AT, owner).start()

        @pl.when(at_home)
        def _():
            gtile[...] = gsend[...]

    gram(FIRST[0])
    x_wait("m1")
    x_onward("m1")
    x_wait("p1")
    x_onward("p1")
    x_wait("y0")
    for n in FIRST[1:]:
        gram(n)
    for n in FIRST:
        reduce_x(n)
    x_pass("m2", "p2")
    x_onward("y0")
    x_wait("y1")
    for n in SECOND:
        gram(n)
    for place in (0, 2):
        reduce_y(place)
    for n in SECOND:
        reduce_x(n)

    @pl.when(lax.rem(yh, 2) == 0)
    def _():
        deliver()

    x_wait("y2")
    for n in LAST:
        gram(n)
    x_pass("p3")
    for n in LAST:
        reduce_x(n)
    for place in (1, 3):
        reduce_y(place)
    x_pass("m3", "n1")

    @pl.when(lax.rem(yh, 2) == 1)
    def _():
        deliver()

    @pl.when(jnp.logical_not(at_home))
    def _():
        arrived(gtile, G_AT)

    tile = gtile[...]
    abuf[me] = tile
    bbuf[r, mine] = tile

    def b_send(at, steps, name, s):
        number = B_AT + NUMBER[name]
        device = link["y"] if at == "y" else (at_row(0, steps), c)
        copy(bbuf.at[s, mine], bbuf.at[s, mine], number, number, device).start()

    def b_share(s):
        copy(bbuf.at[s, mine], bbuf.at[s, mine], BC_AT + s, BC_AT + s, sibling).start()

    def b_pass(*names):
        for name in names:
            s = at_row(*KIND[name])
            arrived(bbuf.at[s, mine], B_AT + NUMBER[name])
            b_share(s)
            for at, steps, new in PANEL.get(name, ()):
                b_send(at, steps, new, s)

    def beside(dx, dy):
        return lax.rem(yh + dy, YH) * X + lax.rem(x + dx, X)

    def a_spread(s, first):
        for i, dx in enumerate((1, 3, 2)):
            copy(abuf.at[s], abuf.at[s], A_AT + first + i, A_AT + s, (r, at_col(dx, 0))).start()

    def a_pass(number, dy):
        s = beside(0, YH - dy)
        arrived(abuf.at[s], A_AT + s)
        a_spread(s, 3 + 3 * number)

    for at, steps, name in (("z", 2, "m2"), ("z", -2, "p2"), ("z", 1, "m1"), ("z", -1, "p1"), ("y", 0, "y0")):
        b_send(at, steps, name, r)
    for j, dy in enumerate((1, 3, 2)):
        copy(abuf.at[me], abuf.at[me], A_AT + j, A_AT + me, (r, at_col(0, dy))).start()
    a_spread(me, 3)
    b_share(r)
    x_pass("y3")
    b_pass("m1", "p1", "m2", "p2")
    a_pass(1, 1)
    a_pass(2, 3)
    a_pass(3, 2)
    b_pass("m3", "p3", "q4", "y0", "n1", "y1", "n2", "y2", "n3", "y3", "r4")
    for dx in (1, 3, 2):
        for dy in range(YH):
            s = beside(dx, dy)
            arrived(abuf.at[s], A_AT + s)

    squared = jnp.zeros((half, rows), jnp.float32)
    for s in range(N_ROW):
        arrived(bbuf.at[s, other], BC_AT + s)
        squared = squared + jnp.dot(abuf[s], bbuf[s], preferred_element_type=jnp.float32)
    fbuf[me, mine] = (coef_b * tile.astype(jnp.float32) + coef_c * squared).astype(jnp.bfloat16)

    def f_share(s):
        copy(fbuf.at[s, mine], fbuf.at[s, mine], FC_AT + s, FC_AT + s, sibling).start()

    def f_spread(s, first):
        for i, dx in enumerate((1, 3, 2)):
            copy(
                fbuf.at[s, mine], fbuf.at[s, mine], F_AT + first + i, F_AT + s, (r, at_col(dx, 0))
            ).start()

    def f_apply(dx):
        for dy in range(YH):
            s = beside(dx, dy)
            arrived(fbuf.at[s, other], FC_AT + s)
            acc[...] += jnp.dot(fbuf[s], xbuf[s], preferred_element_type=jnp.float32)

    for j, dy in enumerate((1, 3, 2)):
        copy(fbuf.at[me, mine], fbuf.at[me, mine], F_AT + j, F_AT + me, (r, at_col(0, dy))).start()
    f_spread(me, 3)
    f_share(me)
    acc[...] = coef_a * x_ref[...].astype(jnp.float32)
    for name in ("q4", "n2", "n3", "r4"):
        x_wait(name)
    for j, dy in enumerate((1, 3, 2)):
        s = beside(0, YH - dy)
        arrived(fbuf.at[s, mine], F_AT + s)
        f_share(s)
        f_spread(s, 6 + 3 * j)
    done = 0
    for dx in (1, 3, 2):
        for dy in range(YH):
            s = beside(dx, dy)
            arrived(fbuf.at[s, mine], F_AT + s)
            f_share(s)
        f_apply(done)
        done = dx
    f_apply(done)
    o_ref[...] = (scale * acc[...]).astype(o_ref.dtype)

    for number in range(15):
        left(x_ref, X_AT + number)
        left(abuf.at[0], A_AT + number)
        left(abuf.at[0], B_AT + number)
        left(abuf.at[0], F_AT + number)
    for place in range(YH):

        @pl.when(yh != place)
        def _():
            left(ysend.at[place], Y_AT + place)

    @pl.when(jnp.logical_not(at_home))
    def _():
        left(gsend, G_AT)

    def all_left(s, carry):
        left(cbuf.at[s], CORE_AT + s)
        left(cbuf.at[s], BC_AT + s)
        left(cbuf.at[s], FC_AT + s)

        @pl.when(s // YH != x)
        def _():
            left(xsum.at[s], XR_AT + s)

        return carry

    lax.fori_loop(0, N_ROW, all_left, 0)


def solution(mesh):
    def step(iterate):
        rows, width = iterate.shape
        half, n = rows // 2, width * mesh.shape["col"]
        bf16 = jnp.bfloat16

        def body(*refs):
            kernel(math.sqrt(n), *refs)

        return pl.pallas_call(
            body,
            out_shape=jax.ShapeDtypeStruct((rows, width), bf16),
            in_specs=[pl.BlockSpec(memory_space=pltpu.VMEM)],
            out_specs=pl.BlockSpec(memory_space=pltpu.VMEM),
            scratch_shapes=[
                pltpu.VMEM((N_ROW, rows, width), bf16),
                pltpu.VMEM((N_ROW, rows, rows), bf16),
                pltpu.VMEM((N_ROW, half, rows), bf16),
                pltpu.VMEM((N_ROW, half, rows), bf16),
                pltpu.VMEM((X, YH, half, rows), bf16),
                pltpu.VMEM((YH, half, rows), bf16),
                pltpu.VMEM((YH, half, rows), bf16),
                pltpu.VMEM((half, rows), bf16),
                pltpu.VMEM((half, rows), bf16),
                pltpu.VMEM((N_ROW, half, rows), bf16),
                pltpu.VMEM((N_ROW, rows, rows), bf16),
                pltpu.VMEM((N_ROW, rows, rows), bf16),
                pltpu.VMEM((rows, width), jnp.float32),
                pltpu.SemaphoreType.DMA((N_SEM,)),
                pltpu.SemaphoreType.DMA((N_SEM,)),
            ],
            compiler_params=pltpu.CompilerParams(
                collective_id=0, has_side_effects=True, vmem_limit_bytes=48 << 20
            ),
            cost_estimate=pl.CostEstimate(
                flops=2 * rows * N_ROW * rows * (2 * width + half), bytes_accessed=4 * rows * width, transcendentals=0
            ),
        )(iterate)

    return jax.shard_map(
        step, mesh=mesh, in_specs=(P("row", "col"),), out_specs=P("row", "col"), check_vma=False
    )
```

time: 103 us -> 104 us (level); the launches traced: 103 us -> 103 us
  no operation moved by 1% of the time
where the time goes in v3:
time: 104 us; the launch traced here: 103 us
  Pallas kernels  101 us (97%)
  local copies, waits for them, and re-layouts  1.67 us (2%)
    pallas_call x1, Pallas kernels, step(): pl.pallas_call(body, out_shape=jax.ShapeDtypeStruct((rows, width), bf16),...  101 us

profile of v3, /device:TPU:1, one launch (start us, length us, event | category | flops | bytes accessed | tf_op | source)
XLA Modules:
  0.0 102.7 jit_solution(8910104131492385281)
XLA Ops:
  0.0 0.0 copy-start
  0.0 1.0 copy-done
  1.0 101.1 %shard_map.17 = bf16[224,576]{1,0:T(8,128)(2,1)S(1)} custom-call(bf16[224,576]{1,0:T(8,128)(2,1)S(1)} %copy-done), custom_call_target="tpu_custom_call" | custom-call | flops 2029518848 | bytes 516096 | tf_op jit(solution)/shard_map/pallas_call | solution.py:371
  102.0 0.7 copy.3
Async XLA Ops:
  0.0 1.0 copy-start

commit v4 on v3

--- a/solution.py
+++ b/solution.py
@@ -1,3 +1,4 @@
+import functools
 import math
 
 import jax
@@ -16,7 +17,7 @@
 N_ROW = 2 * Z
 
 X_AT = 0
-CORE_AT = X_AT + 15
+CORE_AT = X_AT + 16
 XR_AT = CORE_AT + 16
 Y_AT = XR_AT + 16
 G_AT = Y_AT + 4
@@ -33,10 +34,11 @@
     "y0": (1, 0), "y1": (1, 1), "y2": (1, 2), "y3": (1, 3), "r4": (1, 4), "n1": (1, -1), "n2": (1, -2), "n3": (1, -3),
 }
 NUMBER = {name: i for i, name in enumerate(KIND)}
+HALVES = {"y2a": ("y2", NUMBER["y2"], 0), "y2b": ("y2", len(KIND), 1)}
 ONWARD = {
     "m1": (("u", "m2"),), "m2": (("u", "m3"),), "m3": (("y", "n3"),),
-    "p1": (("d", "p2"), ("y", "y1")), "p2": (("d", "p3"), ("y", "y2")), "p3": (("d", "q4"), ("y", "y3")),
-    "y0": (("u", "n1"),), "n1": (("u", "n2"),), "y3": (("d", "r4"),),
+    "p1": (("d", "p2"), ("y", "y1")), "p2": (("d", "p3"), ("y", "y2a")), "p3": (("d", "q4"), ("y", "y3")),
+    "y0": (("u", "n1"),), "y1": (("d", "y2b"),), "n1": (("u", "n2"),), "y3": (("d", "r4"),),
 }
 PANEL = {
     "m1": (("y", 0, "n1"),), "p1": (("y", 0, "y1"),),
@@ -53,6 +55,7 @@
 FIRST = (0, 2, 4, 6, 8, 10, 12, 14)
 SECOND = (1, 3, 5, 7, 9, 11, 13)
 LAST = (15,)
+TURN = tuple(2 if n in LAST else n % 2 for n in range(16))
 
 
 def pick(index, values):
@@ -121,18 +124,22 @@
     def left(src, sent):
         copy(src, src, sent, sent, sibling).wait_send()
 
-    def x_send(src, at, name, s):
-        number = X_AT + NUMBER[name]
-        copy(src, xbuf.at[s], number, number, link[at]).start()
-
-    def x_wait(name):
+    def x_part(name, s):
+        if name in HALVES:
+            kind, number, part = HALVES[name]
+            return xbuf.at[s, pl.ds(part * half, half)], X_AT + number
+        return xbuf.at[s], X_AT + NUMBER[name]
+
+    def x_wait(*names):
+        for name in names:
+            arrived(*x_part(name, at_row(*KIND[HALVES[name][0] if name in HALVES else name])))
+
+    def x_onward(name, *only):
         s = at_row(*KIND[name])
-        arrived(xbuf.at[s], X_AT + NUMBER[name])
-
-    def x_onward(name):
-        s = at_row(*KIND[name])
-        for at, new in ONWARD.get(name, ()):
-            x_send(xbuf.at[s], at, new, s)
+        for at, new in ONWARD[name]:
+            if not only or new in only:
+                part, number = x_part(new, s)
+                copy(part, part, number, number, link[at]).start()
 
     def x_pass(*names):
         for name in names:
@@ -140,7 +147,7 @@
             x_onward(name)
 
     for at, name in (("u", "m1"), ("d", "p1"), ("y", "y0")):
-        x_send(x_ref, at, name, r)
+        copy(x_ref, xbuf.at[r], X_AT + NUMBER[name], X_AT + NUMBER[name], link[at]).start()
     xbuf[r] = x_ref[...]
 
     def gram(n):
@@ -205,9 +212,11 @@
         gram(n)
     for n in FIRST:
         reduce_x(n)
-    x_pass("m2", "p2")
+    x_wait("m2", "p2")
+    x_onward("p2", "y2a")
+    x_pass("y1")
+    x_onward("m2")
     x_onward("y0")
-    x_wait("y1")
     for n in SECOND:
         gram(n)
     for place in (0, 2):
@@ -219,27 +228,14 @@
     def _():
         deliver()
 
-    x_wait("y2")
+    x_wait("y2a", "y2b")
     for n in LAST:
         gram(n)
-    x_pass("p3")
+    x_onward("p2", "p3")
     for n in LAST:
         reduce_x(n)
     for place in (1, 3):
         reduce_y(place)
-    x_pass("m3", "n1")
-
-    @pl.when(lax.rem(yh, 2) == 1)
-    def _():
-        deliver()
-
-    @pl.when(jnp.logical_not(at_home))
-    def _():
-        arrived(gtile, G_AT)
-
-    tile = gtile[...]
-    abuf[me] = tile
-    bbuf[r, mine] = tile
 
     def b_send(at, steps, name, s):
         number = B_AT + NUMBER[name]
@@ -269,18 +265,50 @@
         arrived(abuf.at[s], A_AT + s)
         a_spread(s, 3 + 3 * number)
 
-    for at, steps, name in (("z", 2, "m2"), ("z", -2, "p2"), ("z", 1, "m1"), ("z", -1, "p1"), ("y", 0, "y0")):
-        b_send(at, steps, name, r)
-    for j, dy in enumerate((1, 3, 2)):
-        copy(abuf.at[me], abuf.at[me], A_AT + j, A_AT + me, (r, at_col(0, dy))).start()
-    a_spread(me, 3)
-    b_share(r)
+    def start():
+        @pl.when(jnp.logical_not(at_home))
+        def _():
+            arrived(gtile, G_AT)
+
+        abuf[me] = gtile[...]
+        bbuf[r, mine] = gtile[...]
+        for at, steps, name in (("z", 2, "m2"), ("z", -2, "p2"), ("z", 1, "m1"), ("z", -1, "p1"), ("y", 0, "y0")):
+            b_send(at, steps, name, r)
+        for j, dy in enumerate((1, 3, 2)):
+            copy(abuf.at[me], abuf.at[me], A_AT + j, A_AT + me, (r, at_col(0, dy))).start()
+        a_spread(me, 3)
+        b_share(r)
+
+    def turn(side, steps):
+        return pick(lax.rem(side + 2, 2) * Z + lax.rem(steps + 2 * Z, Z), [TURN[n] for n, a in found])
+
+    def turn_of(row, s):
+        return turn(s // Z - row // Z, lax.rem(s, Z) - lax.rem(row, Z))
+
+    def panels(now):
+        for name in ("m1", "p1", "m2", "p2"):
+            pl.when(turn_of(at_row(*KIND[name]), me) == now)(functools.partial(b_pass, name))
+        for number, dy in enumerate((1, 3, 2), 1):
+            pl.when(turn_of(r, beside(0, YH - dy)) == now)(functools.partial(a_pass, number, dy))
+        for name in ("m3", "p3", "q4"):
+            pl.when(turn_of(at_row(*KIND[name]), me) == now)(functools.partial(b_pass, name))
+
+    mine_is = turn_of(r, me)
+    pl.when(mine_is == 0)(start)
+    x_pass("m3", "n1")
+
+    @pl.when(lax.rem(yh, 2) == 1)
+    def _():
+        deliver()
+
+    panels(0)
+    x_pass("p3")
+    pl.when(mine_is == 1)(start)
+    pl.when(mine_is == 2)(start)
+    panels(1)
     x_pass("y3")
-    b_pass("m1", "p1", "m2", "p2")
-    a_pass(1, 1)
-    a_pass(2, 3)
-    a_pass(3, 2)
-    b_pass("m3", "p3", "q4", "y0", "n1", "y1", "n2", "y2", "n3", "y3", "r4")
+    panels(2)
+    b_pass("y0", "n1", "y1", "n2", "y2", "n3", "y3", "r4")
     for dx in (1, 3, 2):
         for dy in range(YH):
             s = beside(dx, dy)
@@ -290,7 +318,7 @@
     for s in range(N_ROW):
         arrived(bbuf.at[s, other], BC_AT + s)
         squared = squared + jnp.dot(abuf[s], bbuf[s], preferred_element_type=jnp.float32)
-    fbuf[me, mine] = (coef_b * tile.astype(jnp.float32) + coef_c * squared).astype(jnp.bfloat16)
+    fbuf[me, mine] = (coef_b * gtile[...].astype(jnp.float32) + coef_c * squared).astype(jnp.bfloat16)
 
     def f_share(s):
         copy(fbuf.at[s, mine], fbuf.at[s, mine], FC_AT + s, FC_AT + s, sibling).start()
@@ -330,8 +358,10 @@
     f_apply(done)
     o_ref[...] = (scale * acc[...]).astype(o_ref.dtype)
 
+    for number in range(16):
+        split = number in [n for kind, n, part in HALVES.values()]
+        left(x_ref.at[pl.ds(0, half)] if split else x_ref, X_AT + number)
     for number in range(15):
-        left(x_ref, X_AT + number)
         left(abuf.at[0], A_AT + number)
         left(abuf.at[0], B_AT + number)
         left(abuf.at[0], F_AT + number)

time: 104 us -> 108 us (1.038)
  the two profiles are of different devices: /device:TPU:1 before, /device:TPU:13 now
where the time goes in v4:
time: 108 us
  Pallas kernels  106 us (98%)
  local copies, waits for them, and re-layouts  1.67 us (2%)
    pallas_call x1, Pallas kernels, step(): pl.pallas_call(body, out_shape=jax.ShapeDtypeStruct((rows, width), bf16),...  106 us

profile of v4, /device:TPU:13, one launch (start us, length us, event | category | flops | bytes accessed | tf_op | source)
XLA Modules:
  0.0 108.1 jit_solution(6355014579168715628)
XLA Ops:
  0.0 0.0 copy-start
  0.0 1.0 copy-done
  1.0 106.4 %shard_map.17 = bf16[224,576]{1,0:T(8,128)(2,1)S(1)} custom-call(bf16[224,576]{1,0:T(8,128)(2,1)S(1)} %copy-done), custom_call_target="tpu_custom_call" | custom-call | flops 2029518848 | bytes 516096 | tf_op jit(solution)/shard_map/pallas_call | solution.py:401
  107.4 0.7 copy.3
Async XLA Ops:
  0.0 1.0 copy-start

commit v5 on v3

--- a/solution.py
+++ b/solution.py
@@ -1,3 +1,4 @@
+import functools
 import math
 
 import jax
@@ -16,7 +17,7 @@
 N_ROW = 2 * Z
 
 X_AT = 0
-CORE_AT = X_AT + 15
+CORE_AT = X_AT + 45
 XR_AT = CORE_AT + 16
 Y_AT = XR_AT + 16
 G_AT = Y_AT + 4
@@ -33,10 +34,14 @@
     "y0": (1, 0), "y1": (1, 1), "y2": (1, 2), "y3": (1, 3), "r4": (1, 4), "n1": (1, -1), "n2": (1, -2), "n3": (1, -3),
 }
 NUMBER = {name: i for i, name in enumerate(KIND)}
+MAIN, CUT = 512, 128
+BOTH = (0, 1)
 ONWARD = {
-    "m1": (("u", "m2"),), "m2": (("u", "m3"),), "m3": (("y", "n3"),),
-    "p1": (("d", "p2"), ("y", "y1")), "p2": (("d", "p3"), ("y", "y2")), "p3": (("d", "q4"), ("y", "y3")),
-    "y0": (("u", "n1"),), "n1": (("u", "n2"),), "y3": (("d", "r4"),),
+    "m1": (("u", "m2", BOTH),), "m2": (("u", "m3", BOTH),),
+    "p1": (("d", "p2", BOTH), ("y", "y1", BOTH)), "p2": (("d", "p3", BOTH), ("y", "y2", (0,))),
+    "p3": (("d", "q4", BOTH), ("y", "y3", BOTH)),
+    "y0": (("u", "n1", BOTH),), "y1": (("d", "y2", (1,)),), "y3": (("d", "r4", BOTH),),
+    "n1": (("u", "n2", BOTH),), "n2": (("u", "n3", BOTH),),
 }
 PANEL = {
     "m1": (("y", 0, "n1"),), "p1": (("y", 0, "y1"),),
@@ -61,9 +66,10 @@
 
 
 def kernel(
-    scale, x_ref, o_ref, xbuf, pbuf, cbuf, xsum, xrecv, ysend, yrecv, gsend, gtile, abuf, bbuf, fbuf, acc, send_sem, recv_sem
+    scale, x_ref, o_ref, xown, xmain, xpack, xtail, pbuf, cbuf, xsum, xrecv, ysend, yrecv, gsend, gtile, abuf, bbuf, fbuf, acc, fetch_sem, send_sem, recv_sem
 ):
-    rows, half = x_ref.shape[0], x_ref.shape[0] // 2
+    rows, width = x_ref.shape
+    half = rows // 2
     r, c = lax.axis_index("row"), lax.axis_index("col")
     yl, z = r // Z, lax.rem(r, Z)
     x, yh, k = c // (2 * YH), lax.rem(c // 2, YH), lax.rem(c, 2)
@@ -97,6 +103,8 @@
     source = (from_row, pick(from_me, [n for n, a in found]) * 2 + k)
     at_home = jnp.logical_and(to_row == r, to == me)
 
+    fetch = pltpu.make_async_copy(x_ref, xown, fetch_sem)
+    fetch.start()
     barrier = pltpu.get_barrier_semaphore()
     partners = [*link.values(), sibling]
     partners += [(r, at_col(i, 0)) for i in range(1, X)] + [(r, at_col(0, j)) for j in range(1, YH)]
@@ -121,33 +129,57 @@
     def left(src, sent):
         copy(src, src, sent, sent, sibling).wait_send()
 
-    def x_send(src, at, name, s):
-        number = X_AT + NUMBER[name]
-        copy(src, xbuf.at[s], number, number, link[at]).start()
-
-    def x_wait(name):
-        s = at_row(*KIND[name])
-        arrived(xbuf.at[s], X_AT + NUMBER[name])
-
-    def x_onward(name):
-        s = at_row(*KIND[name])
-        for at, new in ONWARD.get(name, ()):
-            x_send(xbuf.at[s], at, new, s)
+    side = width - MAIN
+
+    def pack(s):
+        xpack[s, :, pl.ds(0, side)] = xtail[s, pl.ds(0, half), :]
+        xpack[s, :, pl.ds(side, side)] = xtail[s, pl.ds(half, half), :]
+
+    def unpack(*names):
+        for name in names:
+            s = at_row(*KIND[name])
+            xtail[s, pl.ds(0, half), :] = xpack[s, :, pl.ds(0, side)]
+            xtail[s, pl.ds(half, half), :] = xpack[s, :, pl.ds(side, side)]
+
+    def x_pieces(name, s, part):
+        number = X_AT + 3 * NUMBER[name]
+        if part == 0:
+            return [(xmain.at[s, pl.ds(0, CUT)], number)]
+        return [(xmain.at[s, pl.ds(CUT, rows - CUT)], number + 1), (xpack.at[s], number + 2)]
+
+    def x_send(at, name, s, part):
+        for piece, number in x_pieces(name, s, part):
+            copy(piece, piece, number, number, link[at]).start()
+
+    def x_wait(name, part):
+        for piece, number in x_pieces(name, at_row(*KIND[name]), part):
+            arrived(piece, number)
+
+    def x_onward(name, part, *only):
+        for at, new, parts in ONWARD[name]:
+            if part in parts and (not only or new in only):
+                x_send(at, new, at_row(*KIND[name]), part)
 
     def x_pass(*names):
-        for name in names:
-            x_wait(name)
-            x_onward(name)
-
-    for at, name in (("u", "m1"), ("d", "p1"), ("y", "y0")):
-        x_send(x_ref, at, name, r)
-    xbuf[r] = x_ref[...]
+        for part in BOTH:
+            for name in names:
+                x_wait(name, part)
+                x_onward(name, part)
+
+    fetch.wait()
+    xmain[r] = xown[:, pl.ds(0, MAIN)]
+    xtail[r] = xown[:, pl.ds(MAIN, side)]
+    pack(r)
+    for part in BOTH:
+        for at, name in (("u", "m1"), ("d", "p1"), ("y", "y0")):
+            x_send(at, name, r, part)
 
     def gram(n):
         a, b = BLOCKS[n]
-        product = lax.dot_general(
-            xbuf[at_row(*a)], xbuf[at_row(*b)], (((1,), (1,)), ((), ())), preferred_element_type=jnp.float32
-        )
+        a, b = at_row(*a), at_row(*b)
+        across = (((1,), (1,)), ((), ()))
+        product = lax.dot_general(xmain[a], xmain[b], across, preferred_element_type=jnp.float32)
+        product = product + lax.dot_general(xtail[a], xtail[b], across, preferred_element_type=jnp.float32)
         pbuf[n] = product.astype(jnp.bfloat16)
         copy(pbuf.at[n, other], cbuf.at[n], CORE_AT + n, CORE_AT + n, sibling).start()
 
@@ -164,6 +196,16 @@
                 xsum.at[n], xrecv.at[apart, place], XR_AT + n, XR_AT + apart * YH + place,
                 (r, to * (2 * YH) + yh * 2 + k),
             ).start()
+
+    def grams_and_sums(numbers, before):
+        pending = list(before)
+        for n in numbers:
+            gram(n)
+            pending.append(n)
+            if len(pending) > 3:
+                reduce_x(pending.pop(0))
+        for n in pending:
+            reduce_x(n)
 
     def reduce_y(place):
         total = xsum[x * YH + place].astype(jnp.float32)
@@ -196,50 +238,42 @@
             gtile[...] = gsend[...]
 
     gram(FIRST[0])
-    x_wait("m1")
-    x_onward("m1")
-    x_wait("p1")
-    x_onward("p1")
-    x_wait("y0")
-    for n in FIRST[1:]:
-        gram(n)
-    for n in FIRST:
-        reduce_x(n)
-    x_pass("m2", "p2")
-    x_onward("y0")
-    x_wait("y1")
-    for n in SECOND:
-        gram(n)
+    for part in BOTH:
+        for name in ("m1", "p1", "y0"):
+            x_wait(name, part)
+            if name != "y0":
+                x_onward(name, part)
+    unpack("m1", "p1", "y0")
+    grams_and_sums(FIRST[1:], FIRST[:1])
+    for part in BOTH:
+        x_wait("m2", part)
+        x_wait("p2", part)
+        x_onward("p2", part, "y2")
+        x_wait("y1", part)
+        x_onward("y1", part)
+    for part in BOTH:
+        x_onward("m2", part)
+        x_onward("y0", part)
+    unpack("m2", "p2", "y1")
+    grams_and_sums(SECOND, ())
     for place in (0, 2):
         reduce_y(place)
-    for n in SECOND:
+    for part in BOTH:
+        x_wait("y2", part)
+    unpack("y2")
+    for n in LAST:
+        gram(n)
+    for part in BOTH:
+        x_onward("p2", part, "p3")
+    for n in LAST:
         reduce_x(n)
 
     @pl.when(lax.rem(yh, 2) == 0)
     def _():
         deliver()
 
-    x_wait("y2")
-    for n in LAST:
-        gram(n)
-    x_pass("p3")
-    for n in LAST:
-        reduce_x(n)
     for place in (1, 3):
         reduce_y(place)
-    x_pass("m3", "n1")
-
-    @pl.when(lax.rem(yh, 2) == 1)
-    def _():
-        deliver()
-
-    @pl.when(jnp.logical_not(at_home))
-    def _():
-        arrived(gtile, G_AT)
-
-    tile = gtile[...]
-    abuf[me] = tile
-    bbuf[r, mine] = tile
 
     def b_send(at, steps, name, s):
         number = B_AT + NUMBER[name]
@@ -269,17 +303,30 @@
         arrived(abuf.at[s], A_AT + s)
         a_spread(s, 3 + 3 * number)
 
+    x_pass("n1", "p3")
+
+    @pl.when(lax.rem(yh, 2) == 1)
+    def _():
+        deliver()
+
+
+    @pl.when(jnp.logical_not(at_home))
+    def _():
+        arrived(gtile, G_AT)
+
+    abuf[me] = gtile[...]
+    bbuf[r, mine] = gtile[...]
     for at, steps, name in (("z", 2, "m2"), ("z", -2, "p2"), ("z", 1, "m1"), ("z", -1, "p1"), ("y", 0, "y0")):
         b_send(at, steps, name, r)
     for j, dy in enumerate((1, 3, 2)):
         copy(abuf.at[me], abuf.at[me], A_AT + j, A_AT + me, (r, at_col(0, dy))).start()
     a_spread(me, 3)
     b_share(r)
-    x_pass("y3")
     b_pass("m1", "p1", "m2", "p2")
     a_pass(1, 1)
     a_pass(2, 3)
     a_pass(3, 2)
+    x_pass("y3", "n2")
     b_pass("m3", "p3", "q4", "y0", "n1", "y1", "n2", "y2", "n3", "y3", "r4")
     for dx in (1, 3, 2):
         for dy in range(YH):
@@ -290,7 +337,7 @@
     for s in range(N_ROW):
         arrived(bbuf.at[s, other], BC_AT + s)
         squared = squared + jnp.dot(abuf[s], bbuf[s], preferred_element_type=jnp.float32)
-    fbuf[me, mine] = (coef_b * tile.astype(jnp.float32) + coef_c * squared).astype(jnp.bfloat16)
+    fbuf[me, mine] = (coef_b * gtile[...].astype(jnp.float32) + coef_c * squared).astype(jnp.bfloat16)
 
     def f_share(s):
         copy(fbuf.at[s, mine], fbuf.at[s, mine], FC_AT + s, FC_AT + s, sibling).start()
@@ -305,15 +352,18 @@
         for dy in range(YH):
             s = beside(dx, dy)
             arrived(fbuf.at[s, other], FC_AT + s)
-            acc[...] += jnp.dot(fbuf[s], xbuf[s], preferred_element_type=jnp.float32)
+            acc[:, pl.ds(0, MAIN)] += jnp.dot(fbuf[s], xmain[s], preferred_element_type=jnp.float32)
+            acc[:, pl.ds(MAIN, side)] += jnp.dot(fbuf[s], xtail[s], preferred_element_type=jnp.float32)
 
     for j, dy in enumerate((1, 3, 2)):
         copy(fbuf.at[me, mine], fbuf.at[me, mine], F_AT + j, F_AT + me, (r, at_col(0, dy))).start()
     f_spread(me, 3)
     f_share(me)
-    acc[...] = coef_a * x_ref[...].astype(jnp.float32)
-    for name in ("q4", "n2", "n3", "r4"):
-        x_wait(name)
+    acc[...] = coef_a * xown[...].astype(jnp.float32)
+    for name in ("m3", "q4", "n3", "r4"):
+        for part in BOTH:
+            x_wait(name, part)
+    unpack("m3", "p3", "q4", "y3", "n1", "n2", "n3", "r4")
     for j, dy in enumerate((1, 3, 2)):
         s = beside(0, YH - dy)
         arrived(fbuf.at[s, mine], F_AT + s)
@@ -330,8 +380,11 @@
     f_apply(done)
     o_ref[...] = (scale * acc[...]).astype(o_ref.dtype)
 
+    for name in KIND:
+        for part in BOTH:
+            for piece, number in x_pieces(name, 0, part):
+                left(piece, number)
     for number in range(15):
-        left(x_ref, X_AT + number)
         left(abuf.at[0], A_AT + number)
         left(abuf.at[0], B_AT + number)
         left(abuf.at[0], F_AT + number)
@@ -371,10 +424,13 @@
         return pl.pallas_call(
             body,
             out_shape=jax.ShapeDtypeStruct((rows, width), bf16),
-            in_specs=[pl.BlockSpec(memory_space=pltpu.VMEM)],
+            in_specs=[pl.BlockSpec(memory_space=pl.ANY)],
             out_specs=pl.BlockSpec(memory_space=pltpu.VMEM),
             scratch_shapes=[
-                pltpu.VMEM((N_ROW, rows, width), bf16),
+                pltpu.VMEM((rows, width), bf16),
+                pltpu.VMEM((N_ROW, rows, MAIN), bf16),
+                pltpu.VMEM((N_ROW, half, 2 * (width - MAIN)), bf16),
+                pltpu.VMEM((N_ROW, rows, width - MAIN), bf16),
                 pltpu.VMEM((N_ROW, rows, rows), bf16),
                 pltpu.VMEM((N_ROW, half, rows), bf16),
                 pltpu.VMEM((N_ROW, half, rows), bf16),
@@ -387,6 +443,7 @@
                 pltpu.VMEM((N_ROW, rows, rows), bf16),
                 pltpu.VMEM((N_ROW, rows, rows), bf16),
                 pltpu.VMEM((rows, width), jnp.float32),
+                pltpu.SemaphoreType.DMA(()),
                 pltpu.SemaphoreType.DMA((N_SEM,)),
                 pltpu.SemaphoreType.DMA((N_SEM,)),
             ],

time: 104 us -> 96.1 us (0.924)
  Pallas kernels: 101 us -> 92.8 us
    pallas_call x1, Pallas kernels: 101 us -> 92.8 us  [step(): pl.pallas_call(body, out_shape=jax.ShapeDtypeStruct((rows, width), bf16),...]
where the time goes in v5:
time: 96.1 us; the launch traced here: 94.5 us
  Pallas kernels  92.8 us (97%)
  local copies, waits for them, and re-layouts  1.67 us (2%)
    pallas_call x1, Pallas kernels, step(): pl.pallas_call(body, out_shape=jax.ShapeDtypeStruct((rows, width), bf16),...  92.8 us

profile of v5, /device:TPU:1, one launch (start us, length us, event | category | flops | bytes accessed | tf_op | source)
XLA Modules:
  0.0 94.5 jit_solution(15526786091565013075)
XLA Ops:
  0.0 0.0 copy-start
  0.0 1.0 %copy-done = bf16[224,576]{1,0:T(8,128)(2,1)S(1)} copy-done((bf16[224,576]{1,0:T(8,128)(2,1)S(1)}, bf16[224,576]{1,0:T(8,128)(2,1)}, u32[]{:S(2)}) %copy-start) | copy-done | bytes 258072
  1.0 92.8 %shard_map.17 = bf16[224,576]{1,0:T(8,128)(2,1)S(1)} custom-call(bf16[224,576]{1,0:T(8,128)(2,1)S(1)} %copy-done), custom_call_target="tpu_custom_call" | custom-call | flops 2029518848 | bytes 516096 | tf_op jit(solution)/shard_map/pallas_call | solution.py:424
  93.8 0.7 copy.3
Async XLA Ops:
  0.0 1.0 %copy-start = (bf16[224,576]{1,0:T(8,128)(2,1)S(1)}, bf16[224,576]{1,0:T(8,128)(2,1)}, u32[]{:S(2)}) copy-start(bf16[224,576]{1,0:T(8,128)(2,1)} %refs_0_.1) | copy-start | bytes 774148

commit v6 on v5

--- a/solution.py
+++ b/solution.py
@@ -96,11 +96,6 @@
 
     to_row, to = block_at(x * YH + yh)
     owner = (to_row, column(to))
-    apart = {((b[0] - a[0]) % 2, (b[1] - a[1]) % Z): (n, a) for n, (a, b) in enumerate(BLOCKS)}
-    found = [apart[side, steps] for side in range(2) for steps in range(Z)]
-    from_me = lax.rem(me // Z - yl + 2, 2) * Z + lax.rem(lax.rem(me, Z) - z + Z, Z)
-    from_row = at_row(pick(from_me, [a[0] for n, a in found]), 0 - pick(from_me, [a[1] for n, a in found]))
-    source = (from_row, pick(from_me, [n for n, a in found]) * 2 + k)
     at_home = jnp.logical_and(to_row == r, to == me)
 
     fetch = pltpu.make_async_copy(x_ref, xown, fetch_sem)
@@ -111,11 +106,7 @@
     for partner in partners:
         pl.semaphore_signal(barrier, inc=1, device_id=partner, device_id_type=MESH)
 
-    @pl.when(jnp.logical_not(at_home))
-    def _():
-        pl.semaphore_signal(barrier, inc=1, device_id=source, device_id_type=MESH)
-
-    pl.semaphore_wait(barrier, len(partners) + 1 - at_home.astype(jnp.int32))
+    pl.semaphore_wait(barrier, len(partners))
 
     def copy(src, dst, sent, received, device):
         return pltpu.make_async_remote_copy(

time: 96.1 us -> 93.7 us (0.975); the launches traced: 94.5 us -> 93.6 us
  no operation moved by 1% of the time
where the time goes in v6:
time: 93.7 us; the launch traced here: 93.6 us
  Pallas kernels  91.9 us (98%)
  local copies, waits for them, and re-layouts  1.67 us (2%)
    pallas_call x1, Pallas kernels, step(): pl.pallas_call(body, out_shape=jax.ShapeDtypeStruct((rows, width), bf16),...  91.9 us

profile of v6, /device:TPU:1, one launch (start us, length us, event | category | flops | bytes accessed | tf_op | source)
XLA Modules:
  0.0 93.6 jit_solution(13335247958079105299)
XLA Ops:
  0.0 0.0 copy-start
  0.0 1.0 %copy-done = bf16[224,576]{1,0:T(8,128)(2,1)S(1)} copy-done((bf16[224,576]{1,0:T(8,128)(2,1)S(1)}, bf16[224,576]{1,0:T(8,128)(2,1)}, u32[]{:S(2)}) %copy-start) | copy-done | bytes 258072
  1.0 91.9 %shard_map.17 = bf16[224,576]{1,0:T(8,128)(2,1)S(1)} custom-call(bf16[224,576]{1,0:T(8,128)(2,1)S(1)} %copy-done), custom_call_target="tpu_custom_call" | custom-call | flops 2029518848 | bytes 516096 | tf_op jit(solution)/shard_map/pallas_call | solution.py:415
  92.9 0.7 copy.3
Async XLA Ops:
  0.0 1.0 %copy-start = (bf16[224,576]{1,0:T(8,128)(2,1)S(1)}, bf16[224,576]{1,0:T(8,128)(2,1)}, u32[]{:S(2)}) copy-start(bf16[224,576]{1,0:T(8,128)(2,1)} %refs_0_.1) | copy-start | bytes 774148

commit v7 on v6

--- a/solution.py
+++ b/solution.py
@@ -66,7 +66,7 @@
 
 
 def kernel(
-    scale, x_ref, o_ref, xown, xmain, xpack, xtail, pbuf, cbuf, xsum, xrecv, ysend, yrecv, gsend, gtile, abuf, bbuf, fbuf, acc, fetch_sem, send_sem, recv_sem
+    scale, x_ref, o_ref, xown, xmain, xpack, xtail, pbuf, cbuf, xsum, xrecv, ysend, yrecv, gsend, gtile, abuf, bbuf, fbuf, acc, fetch_sem, word_sem, send_sem, recv_sem
 ):
     rows, width = x_ref.shape
     half = rows // 2
@@ -101,12 +101,19 @@
     fetch = pltpu.make_async_copy(x_ref, xown, fetch_sem)
     fetch.start()
     barrier = pltpu.get_barrier_semaphore()
-    partners = [*link.values(), sibling]
-    partners += [(r, at_col(i, 0)) for i in range(1, X)] + [(r, at_col(0, j)) for j in range(1, YH)]
+    outer = (at_row(1, 0), at_col(0, 2 * yl + YH - 1))
+    partners = [*link.values(), sibling, outer, (r, at_col(1, 0)), (r, at_col(X - 1, 0))]
     for partner in partners:
         pl.semaphore_signal(barrier, inc=1, device_id=partner, device_id_type=MESH)
 
     pl.semaphore_wait(barrier, len(partners))
+
+    def tell(number, *devices):
+        for device in devices:
+            pl.semaphore_signal(word_sem.at[number], inc=1, device_id=device, device_id_type=MESH)
+
+    def hear(number, count):
+        pl.semaphore_wait(word_sem.at[number], count)
 
     def copy(src, dst, sent, received, device):
         return pltpu.make_async_remote_copy(
@@ -164,6 +171,8 @@
     for part in BOTH:
         for at, name in (("u", "m1"), ("d", "p1"), ("y", "y0")):
             x_send(at, name, r, part)
+    tell(0, (r, at_col(1, 0)))
+    tell(1, link["y"], outer)
 
     def gram(n):
         a, b = BLOCKS[n]
@@ -229,6 +238,9 @@
             gtile[...] = gsend[...]
 
     gram(FIRST[0])
+    hear(0, 1)
+    hear(1, 2)
+    tell(2, (r, at_col(0, 1)))
     for part in BOTH:
         for name in ("m1", "p1", "y0"):
             x_wait(name, part)
@@ -247,6 +259,7 @@
         x_onward("y0", part)
     unpack("m2", "p2", "y1")
     grams_and_sums(SECOND, ())
+    hear(2, 1)
     for place in (0, 2):
         reduce_y(place)
     for part in BOTH:
@@ -346,29 +359,48 @@
             acc[:, pl.ds(0, MAIN)] += jnp.dot(fbuf[s], xmain[s], preferred_element_type=jnp.float32)
             acc[:, pl.ds(MAIN, side)] += jnp.dot(fbuf[s], xtail[s], preferred_element_type=jnp.float32)
 
+    def f_send(s, number, dx, dy):
+        copy(fbuf.at[s, mine], fbuf.at[s, mine], F_AT + number, F_AT + s, (r, at_col(dx, dy))).start()
+
+    def f_wait(s):
+        arrived(fbuf.at[s, mine], F_AT + s)
+        f_share(s)
+
+    ahead, back = 1 + 2 * k, 3 - 2 * k
+
     for j, dy in enumerate((1, 3, 2)):
-        copy(fbuf.at[me, mine], fbuf.at[me, mine], F_AT + j, F_AT + me, (r, at_col(0, dy))).start()
-    f_spread(me, 3)
+        f_send(me, j, 0, dy)
+    f_send(me, 3, ahead, 0)
+    f_send(me, 4, back, 0)
     f_share(me)
     acc[...] = coef_a * xown[...].astype(jnp.float32)
+    f_wait(beside(back, 0))
+    f_send(beside(back, 0), 5, ahead, 0)
+    f_wait(beside(ahead, 0))
+    for j, dy in enumerate((1, 3, 2)):
+        s = beside(0, YH - dy)
+        f_wait(s)
+        f_send(s, 6 + 3 * j, ahead, 0)
+        f_send(s, 7 + 3 * j, back, 0)
+        if dy == 2:
+            f_send(s, 8 + 3 * j, 2, 0)
+    for j, dy in enumerate((1, 3)):
+        s = beside(back, YH - dy)
+        f_wait(s)
+        f_send(s, 8 + 3 * j, ahead, 0)
+        f_wait(beside(ahead, YH - dy))
     for name in ("m3", "q4", "n3", "r4"):
         for part in BOTH:
             x_wait(name, part)
     unpack("m3", "p3", "q4", "y3", "n1", "n2", "n3", "r4")
-    for j, dy in enumerate((1, 3, 2)):
-        s = beside(0, YH - dy)
-        arrived(fbuf.at[s, mine], F_AT + s)
-        f_share(s)
-        f_spread(s, 6 + 3 * j)
-    done = 0
-    for dx in (1, 3, 2):
-        for dy in range(YH):
-            s = beside(dx, dy)
-            arrived(fbuf.at[s, mine], F_AT + s)
-            f_share(s)
-        f_apply(done)
-        done = dx
-    f_apply(done)
+    f_apply(0)
+    f_wait(beside(back, 2))
+    f_wait(beside(ahead, 2))
+    f_apply(1)
+    for dy in (0, 1, 3, 2):
+        f_wait(beside(2, dy))
+    f_apply(3)
+    f_apply(2)
     o_ref[...] = (scale * acc[...]).astype(o_ref.dtype)
 
     for name in KIND:
@@ -435,6 +467,7 @@
                 pltpu.VMEM((N_ROW, rows, rows), bf16),
                 pltpu.VMEM((rows, width), jnp.float32),
                 pltpu.SemaphoreType.DMA(()),
+                pltpu.SemaphoreType.REGULAR((3,)),
                 pltpu.SemaphoreType.DMA((N_SEM,)),
                 pltpu.SemaphoreType.DMA((N_SEM,)),
             ],

time: 93.7 us -> 91.3 us (0.974)
  Pallas kernels: 91.9 us -> 89.5 us
    pallas_call x1, Pallas kernels: 91.9 us -> 89.5 us  [step(): pl.pallas_call(body, out_shape=jax.ShapeDtypeStruct((rows, width), bf16),...]
where the time goes in v7:
time: 91.3 us; the launch traced here: 91.2 us
  Pallas kernels  89.5 us (98%)
  local copies, waits for them, and re-layouts  1.67 us (2%)
    pallas_call x1, Pallas kernels, step(): pl.pallas_call(body, out_shape=jax.ShapeDtypeStruct((rows, width), bf16),...  89.5 us

profile of v7, /device:TPU:1, one launch (start us, length us, event | category | flops | bytes accessed | tf_op | source)
XLA Modules:
  0.0 91.2 jit_solution(7523110832388711177)
XLA Ops:
  0.0 0.0 copy-start
  0.0 1.0 %copy-done = bf16[224,576]{1,0:T(8,128)(2,1)S(1)} copy-done((bf16[224,576]{1,0:T(8,128)(2,1)S(1)}, bf16[224,576]{1,0:T(8,128)(2,1)}, u32[]{:S(2)}) %copy-start) | copy-done | bytes 258072
  1.0 89.5 %shard_map.17 = bf16[224,576]{1,0:T(8,128)(2,1)S(1)} custom-call(bf16[224,576]{1,0:T(8,128)(2,1)S(1)} %copy-done), custom_call_target="tpu_custom_call" | custom-call | flops 2029518848 | bytes 516096 | tf_op jit(solution)/shard_map/pallas_call | solution.py:447
  90.5 0.7 copy.3
Async XLA Ops:
  0.0 1.0 %copy-start = (bf16[224,576]{1,0:T(8,128)(2,1)S(1)}, bf16[224,576]{1,0:T(8,128)(2,1)}, u32[]{:S(2)}) copy-start(bf16[224,576]{1,0:T(8,128)(2,1)} %refs_0_.1) | copy-start | bytes 774148

commit v8 on v7

--- a/solution.py
+++ b/solution.py
@@ -326,12 +326,12 @@
         copy(abuf.at[me], abuf.at[me], A_AT + j, A_AT + me, (r, at_col(0, dy))).start()
     a_spread(me, 3)
     b_share(r)
-    b_pass("m1", "p1", "m2", "p2")
+    b_pass("m1", "p1", "y0", "m2", "p2")
     a_pass(1, 1)
     a_pass(2, 3)
     a_pass(3, 2)
     x_pass("y3", "n2")
-    b_pass("m3", "p3", "q4", "y0", "n1", "y1", "n2", "y2", "n3", "y3", "r4")
+    b_pass("n1", "y1", "m3", "p3", "q4", "n2", "y2", "n3", "y3", "r4")
     for dx in (1, 3, 2):
         for dy in range(YH):
             s = beside(dx, dy)
@@ -393,13 +393,15 @@
         for part in BOTH:
             x_wait(name, part)
     unpack("m3", "p3", "q4", "y3", "n1", "n2", "n3", "r4")
+    f_wait(beside(2, 0))
     f_apply(0)
     f_wait(beside(back, 2))
     f_wait(beside(ahead, 2))
     f_apply(1)
-    for dy in (0, 1, 3, 2):
-        f_wait(beside(2, dy))
+    f_wait(beside(2, YH - 1))
     f_apply(3)
+    f_wait(beside(2, 1))
+    f_wait(beside(2, 2))
     f_apply(2)
     o_ref[...] = (scale * acc[...]).astype(o_ref.dtype)
 

time: 91.3 us -> 93.4 us (1.023)
  the two profiles are of different devices: /device:TPU:1 before, /device:TPU:8 now
where the time goes in v8:
time: 93.4 us; the launch traced here: 93.2 us
  Pallas kernels  91.6 us (98%)
  local copies, waits for them, and re-layouts  1.67 us (2%)
    pallas_call x1, Pallas kernels, step(): pl.pallas_call(body, out_shape=jax.ShapeDtypeStruct((rows, width), bf16),...  91.6 us

profile of v8, /device:TPU:8, one launch (start us, length us, event | category | flops | bytes accessed | tf_op | source)
XLA Modules:
  0.0 93.2 jit_solution(10466201869782073343)
XLA Ops:
  0.0 0.0 copy-start
  0.0 1.0 %copy-done = bf16[224,576]{1,0:T(8,128)(2,1)S(1)} copy-done((bf16[224,576]{1,0:T(8,128)(2,1)S(1)}, bf16[224,576]{1,0:T(8,128)(2,1)}, u32[]{:S(2)}) %copy-start) | copy-done | bytes 258072
  1.0 91.6 %shard_map.17 = bf16[224,576]{1,0:T(8,128)(2,1)S(1)} custom-call(bf16[224,576]{1,0:T(8,128)(2,1)S(1)} %copy-done), custom_call_target="tpu_custom_call" | custom-call | flops 2029518848 | bytes 516096 | tf_op jit(solution)/shard_map/pallas_call | solution.py:449
  92.5 0.7 copy.3
Async XLA Ops:
  0.0 1.0 %copy-start = (bf16[224,576]{1,0:T(8,128)(2,1)S(1)}, bf16[224,576]{1,0:T(8,128)(2,1)}, u32[]{:S(2)}) copy-start(bf16[224,576]{1,0:T(8,128)(2,1)} %refs_0_.1) | copy-start | bytes 774148
